TPU v7x, 32 devices: a whole 2x2x4 slice. The times are simulated.
32 devices in a mesh: section: 16 (over z, y, core), tensor: 2 (over x).
Axes of the slice: x: 2, y: 2, z: 4, core: 2. Of those that a mesh axis runs over, the one named last changes fastest.
Arguments:
- memory: bfloat16 [2, 12288, 4096], P(None, 'section', 'tensor'), may hold values from -4 to 4
- queries: bfloat16 [4096, 4096], P(('section', 'tensor')), may hold values from -6.5 to 6.5
- out_grad: bfloat16 [4096, 4096], P(('section', 'tensor')), may hold values from -6 to 6
- enc_lengths: int32 [16, 8], replicated, may hold values from 1 to 128, 768 in all within a row
- dec_lengths: int32 [16, 8], replicated, may hold values from 1 to 64, 256 in all within a row
- readers: int32 [16, 8], replicated, may hold values from 0 to 15, as said below
Outputs:
- attended: bfloat16 [4096, 4096], P(('section', 'tensor'))
- query_grad: bfloat16 [4096, 4096], P(('section', 'tensor'))
- memory_grad: bfloat16 [2, 12288, 4096], P(None, 'section', 'tensor')
Inputs may be any that keep to these rules, and one draw needn't show every extreme that they name: `readers`: the reader of example j of encoder device s is (s + k * 2 + 1) modulo 16 for some k < 8; each encoder device names each of its 8 such devices exactly 1 times, so every decoder device is named exactly 8 times.
All inputs are finite; a program needn't handle non-finite values.
Results may differ from a plain program's by a relative error of at most 0.011.
Values may be sent and summed in bfloat16 or wider, within the bound.
A program may use at most 64 MiB of HBM per device.

v0:
```python
import jax
import jax.numpy as jnp
from jax import lax
from jax.sharding import PartitionSpec as P

HD = 128
ENC_MAX = 128
DEC_MAX = 64
PARTNERS = 8


def from_behind(shard, axis, by):
    devices = lax.axis_size(axis)
    return lax.ppermute(shard, axis, [(i, (i + by) % devices) for i in range(devices)])


def exclusive(lengths):
    return jnp.cumsum(lengths, axis=-1) - lengths


def lookup(entries, wanted):
    labels = jnp.arange(entries.shape[0], dtype=jnp.int32)
    hits = wanted[..., None] == labels
    return jnp.sum(jnp.where(hits, entries, 0), axis=-1)


def inverse(slots):
    labels = jnp.arange(slots.shape[0], dtype=jnp.int32)
    hits = slots[None, :] == labels[:, None]
    return jnp.sum(jnp.where(hits, labels[None, :], 0), axis=1)


def segments(lengths, row_count):
    bounds = jnp.cumsum(lengths)
    position = jnp.arange(row_count, dtype=jnp.int32)
    member = jnp.sum((position[:, None] >= bounds[None, :]).astype(jnp.int32), axis=1)
    within = position - lookup(exclusive(lengths), member)
    return (member, within)


def reader_examples(readers, reader, number):
    flattened = readers.reshape(-1)
    is_mine = (flattened == reader).astype(jnp.int32)
    ordinal = jnp.cumsum(is_mine) - is_mine
    labels = jnp.arange(number, dtype=jnp.int32)
    matches = (is_mine[None, :] == 1) & (ordinal[None, :] == labels[:, None])
    everyone = jnp.arange(flattened.shape[0], dtype=jnp.int32)
    return jnp.sum(jnp.where(matches, everyone[None, :], 0), axis=1)


def attend(query_block, grad_block, key_block, value_block, key_valid):
    count, dec_rows, width = query_block.shape
    enc_rows = key_block.shape[1]
    head_count = width // HD
    scaling = HD ** (-0.5)
    query_heads = query_block.reshape(count, dec_rows, head_count, HD)
    grad_heads = grad_block.reshape(count, dec_rows, head_count, HD)
    key_heads = key_block.reshape(count, enc_rows, head_count, HD)
    value_heads = value_block.reshape(count, enc_rows, head_count, HD)
    scores = (
        jnp.einsum("eqhd,ekhd->ehqk", query_heads, key_heads, preferred_element_type=jnp.float32)
        * scaling
    )
    scores = jnp.where(key_valid[:, None, None, :], scores, -jnp.inf)
    highest = jnp.max(scores, axis=3, keepdims=True)
    weights = jnp.exp(scores - highest)
    probabilities = weights / jnp.sum(weights, axis=3, keepdims=True)
    probs_low = probabilities.astype(jnp.bfloat16)
    attended = jnp.einsum(
        "ehqk,ekhd->eqhd", probs_low, value_heads, preferred_element_type=jnp.float32
    ).astype(jnp.bfloat16)
    dprobs = jnp.einsum(
        "eqhd,ekhd->ehqk", grad_heads, value_heads, preferred_element_type=jnp.float32
    )
    row_delta = jnp.sum(probabilities * dprobs, axis=3, keepdims=True)
    dscores = (probabilities * (dprobs - row_delta)).astype(jnp.bfloat16)
    query_grad = (
        jnp.einsum("ehqk,ekhd->eqhd", dscores, key_heads, preferred_element_type=jnp.float32)
        * scaling
    ).astype(jnp.bfloat16)
    key_grad = (
        jnp.einsum("ehqk,eqhd->ekhd", dscores, query_heads, preferred_element_type=jnp.float32)
        * scaling
    ).astype(jnp.bfloat16)
    value_grad = jnp.einsum(
        "ehqk,eqhd->ekhd", probs_low, grad_heads, preferred_element_type=jnp.float32
    ).astype(jnp.bfloat16)
    return (
        attended.reshape(count, dec_rows, width),
        query_grad.reshape(count, dec_rows, width),
        key_grad.reshape(count, enc_rows, width),
        value_grad.reshape(count, enc_rows, width),
    )


def body(memory, queries, out_grad, enc_lengths, dec_lengths, readers):
    section_index = lax.axis_index("section")
    section_count = lax.axis_size("section")
    query_rows, grad_rows = (
        lax.all_to_all(queries, "tensor", split_axis=1, concat_axis=0, tiled=True),
        lax.all_to_all(out_grad, "tensor", split_axis=1, concat_axis=0, tiled=True),
    )
    examples = readers.shape[1]
    spacing = section_count // PARTNERS
    capacity = examples // PARTNERS
    enc_count = memory.shape[1]
    width = memory.shape[2]
    dec_count = query_rows.shape[0]
    labels = jnp.arange(examples, dtype=jnp.int32)
    holder_all = jnp.arange(section_count, dtype=jnp.int32)[:, None]
    partner_all = ((readers - holder_all) % section_count - 1) // spacing
    earlier = labels[:, None] > labels[None, :]
    shared = readers[:, :, None] == readers[:, None, :]
    ordinal_all = jnp.sum((shared & earlier[None, :, :]).astype(jnp.int32), axis=2)
    slot_all = partner_all * capacity + ordinal_all
    reader_ids = reader_examples(readers, section_index, examples)
    recv_slot = lookup(slot_all.reshape(-1), reader_ids)
    slot_example = inverse(recv_slot)
    dec_row = lax.dynamic_index_in_dim(dec_lengths, section_index, 0, keepdims=False)
    dec_member, dec_within = segments(dec_row, dec_count)
    dec_token = lookup(recv_slot, dec_member) * DEC_MAX + dec_within
    dec_offsets = jnp.arange(DEC_MAX, dtype=jnp.int32)
    dec_valid = dec_offsets[None, :] < lookup(dec_row, slot_example)[:, None]
    dec_index = jnp.where(
        dec_valid, lookup(exclusive(dec_row), slot_example)[:, None] + dec_offsets[None, :], 0
    )
    enc_row = lax.dynamic_index_in_dim(enc_lengths, section_index, 0, keepdims=False)
    my_slot = lax.dynamic_index_in_dim(slot_all, section_index, 0, keepdims=False)
    my_chosen = inverse(my_slot)
    enc_member, enc_within = segments(enc_row, enc_count)
    enc_token = lookup(my_slot, enc_member) * ENC_MAX + enc_within
    key_offsets = jnp.arange(ENC_MAX, dtype=jnp.int32)
    local_valid = key_offsets[None, :] < lookup(enc_row, my_chosen)[:, None]
    key_index = jnp.where(
        local_valid, lookup(exclusive(enc_row), my_chosen)[:, None] + key_offsets[None, :], 0
    )
    local_blocks = jnp.take(memory, key_index.reshape(-1), axis=1).reshape(
        2, examples, ENC_MAX, width
    )
    paired = jnp.stack([query_rows, grad_rows])
    zero = jnp.zeros((), memory.dtype)
    dec_blocks = jnp.where(
        dec_valid[None, :, :, None],
        jnp.take(paired, dec_index.reshape(-1), axis=1).reshape(2, examples, DEC_MAX, width),
        zero,
    )
    packed = jnp.where(local_valid[None, :, :, None], local_blocks, zero)
    arrived = []
    for partner in range(PARTNERS):
        arrived.append(from_behind(packed[:, partner], "section", partner * spacing + 1))
    received = jnp.stack(arrived, axis=1)
    slot_enc_len = lookup(lookup(enc_lengths.reshape(-1), reader_ids), slot_example)
    remote_valid = key_offsets[None, :] < slot_enc_len[:, None]
    block_out, block_grad, key_grad, value_grad = attend(
        dec_blocks[0], dec_blocks[1], received[0], received[1], remote_valid
    )
    outgoing = jnp.stack([key_grad, value_grad])
    returned = []
    for partner in range(PARTNERS):
        returned.append(from_behind(outgoing[:, partner], "section", -(partner * spacing + 1)))
    back = jnp.stack(returned, axis=1).reshape(2, examples * ENC_MAX, width)
    memory_grad = jnp.take(back, enc_token, axis=1)
    attended = jnp.take(block_out.reshape(-1, width), dec_token, axis=0)
    query_grad = jnp.take(block_grad.reshape(-1, width), dec_token, axis=0)
    attended_out, query_out = (
        lax.all_to_all(attended, "tensor", split_axis=0, concat_axis=1, tiled=True),
        lax.all_to_all(query_grad, "tensor", split_axis=0, concat_axis=1, tiled=True),
    )
    return (attended_out, query_out, memory_grad)


def solution(mesh):
    placed = (
        P(None, "section", "tensor"),
        P(("section", "tensor"), None),
        P(("section", "tensor"), None),
        P(),
        P(),
        P(),
    )
    return jax.shard_map(
        body,
        mesh=mesh,
        in_specs=placed,
        out_specs=(
            P(("section", "tensor"), None),
            P(("section", "tensor"), None),
            P(None, "section", "tensor"),
        ),
        check_vma=False,
    )
```

profile of v0, /device:TPU:15, one launch (start us, length us, event | category | flops | bytes accessed | tf_op | source)
XLA Modules:
  0.0 580.4 jit_solution(10765943576377632582)
XLA Ops:
  4.0 51.4 %gather_fusion = bf16[1024,2,2048]{2,0,1:T(8,128)(2,1)} fusion(bf16[2,768,2048]{2,1,0:T(8,128)(2,1)} %param.8, s32[1024]{0:T(1024)S(1)} %broadcast_clamp_fusion), kind=kCustom, calls=%fused_computation.2 | custom fusion | bytes 16781312 | tf_op jit(solution)/shard_map/jit(_take)/gather | solution.py:137
  55.4 11.4 %copy.165 = bf16[2,8,128,2048]{2,3,0,1:T(8,128)(2,1)} copy(bf16[2,8,128,2048]{3,2,1,0:T(8,128)(2,1)} %bitcast.166) | data formatting | bytes 16777216 | tf_op jit(solution)/shard_map/jit(_take)/gather | solution.py:137
  66.8 7.5 %select_select_fusion = bf16[2,8,128,2048]{2,3,0,1:T(8,128)(2,1)} fusion(bf16[2,8,128,2048]{2,3,0,1:T(8,128)(2,1)} %copy.165, pred[8,128]{1,0:T(8,128)(4,1)S(1)} %get-tuple-element.54, pred[8,128]{1,0:T(8,128)(4,1)S(1)} %get-tuple-element.53), kind=kLoop, calls=%fused_computation.22 | loop fusion | flops 8388608 | bytes 16779264 | tf_op jit(solution)/shard_map/jit(_where)/select_n | solution.py:147
  74.3 6.1 %slice_bitcast_fusion = (bf16[2,128,2048]{1,2,0:T(8,128)(2,1)}, bf16[2,128,2048]{1,2,0:T(8,128)(2,1)}, bf16[2,128,2048]{1,2,0:T(8,128)(2,1)}, bf16[2,128,2048]{1...) fusion(bf16[2,8,128,2048]{2,3,0,1:T(8,128)(2,1)} %select_select, ...), kind=kLoop, calls=%fused_computation.57 | loop fusion | bytes 16777216 | tf_op jit(solution)/shard_map/squeeze | solution.py:150
  80.5 1.7 collective-permute-start
  82.2 2.6 collective-permute-start.2
  84.8 2.6 collective-permute-start.4
  88.7 3.6 all-to-all-start.1
  95.7 8.8 %all-to-all-done.1 = bf16[128,2,2048]{0,2,1:T(8,128)(2,1)S(1)} async-done(((bf16[128,2,2048]{0,2,1:T(8,128)(2,1)}), bf16[128,2,2048]{0,2,1:T(8,128)(2,1)S(1)}, u32[]{:S(2)}, u32[]{:S(2)}) %all-to-all-start.1) | async-done | bytes 1048608 | tf_op jit(solution)/shard_map/all_to_all | solution.py:101
  104.5 5.6 all-to-all-start
  110.8 2.9 copy.179
  113.7 8.3 %all-to-all-done = bf16[128,2,2048]{0,2,1:T(8,128)(2,1)S(1)} async-done(((bf16[128,2,2048]{0,2,1:T(8,128)(2,1)}), bf16[128,2,2048]{0,2,1:T(8,128)(2,1)S(1)}, u32[]{:S(2)}, u32[]{:S(2)}) %all-to-all-start) | async-done | bytes 1048608 | tf_op jit(solution)/shard_map/all_to_all | solution.py:100
  122.6 1.6 copy.178
  124.2 4.8 pad_maximum_fusion
  129.0 18.5 %gather_fusion.1 = bf16[512,2,2048]{2,1,0:T(2,128)(2,1)} fusion(bf16[2,256,2048]{2,0,1:T(2,128)(2,1)S(1)} %pad_maximum_fusion, s32[1024]{0:T(1024)S(1)} %pad_clamp_fusion.2), kind=kCustom, calls=%fused_computation.3 | custom fusion | bytes 8390656 | tf_op jit(solution)/shard_map/jit(_take)/gather | solution.py:144
  147.5 7.0 %fusion.2 = bf16[2,8,64,2048]{3,2,1,0:T(8,128)(2,1)S(1)} fusion(bf16[2,8,64,2048]{3,0,2,1:T(2,128)(2,1)} %bitcast.169, pred[8,64]{1,0:T(8,128)(4,1)S(1)} %get-tuple-element.52, pred[8,64]{1,0:T(8,128)(4,1)S(1)} %get-tuple-element.51), kind=kLoop, calls=%fused_computation.25 | loop fusion | flops 4194304 | bytes 8389632 | tf_op jit(solution)/shard_map/jit(_where)/select_n | solution.py:142
  157.8 3.2 collective-permute-start.6
  162.4 76.1 %collective-permute-done.2 = bf16[2,128,2048]{1,2,0:T(8,128)(2,1)} collective-permute-done((bf16[2,128,2048]{1,2,0:T(8,128)(2,1)}, bf16[2,128,2048]{1,2,0:T(8,128)(2,1)}, u32[]{:S(2)}, u32[]{:S(2)}) %collective-permute-start.2) | collective-permute-done | bytes 1048608 | tf_op jit(solution)/shard_map/ppermute | solution.py:14
  239.8 21.1 %collective-permute-done.3 = bf16[2,128,2048]{1,2,0:T(8,128)(2,1)} collective-permute-done((bf16[2,128,2048]{1,2,0:T(8,128)(2,1)}, bf16[2,128,2048]{1,2,0:T(8,128)(2,1)}, u32[]{:S(2)}, u32[]{:S(2)}) %collective-permute-start.3) | collective-permute-done | bytes 1048608 | tf_op jit(solution)/shard_map/ppermute | solution.py:14
  267.5 2.9 fusion.42
  270.4 4.2 convert_bitcast_fusion
  274.5 2.6 multiply_reduce_fusion
  277.2 4.0 convolution_convert_fusion
  281.2 2.7 multiply_convert_fusion.2
  283.9 3.0 fusion.13
  286.9 3.5 multiply_convert_fusion
  290.4 1.4 copy.189
  292.3 1.4 copy.184
  293.7 1.9 copy.230
  297.0 4.2 gather_fusion.3
  301.2 1.6 broadcast_select_fusion.1
  302.8 3.8 all-to-all-start.2
  306.6 6.5 %copy.194 = bf16[1,8,128,2048]{3,2,0,1:T(8,128)(2,1)} copy(bf16[1,8,128,2048]{2,3,1,0:T(8,128)(2,1)} %bitcast.178) | data formatting | bytes 8388608 | tf_op jit(solution)/shard_map/stack;reshape | solution.py:157
  313.1 6.4 %copy.193 = bf16[1,8,128,2048]{3,2,0,1:T(8,128)(2,1)} copy(bf16[1,8,128,2048]{2,3,1,0:T(8,128)(2,1)} %bitcast.170) | data formatting | bytes 8388608 | tf_op jit(solution)/shard_map/stack;reshape | solution.py:157
  319.5 5.7 fusion.21
  326.3 3.6 all-to-all-start.3
  330.0 2.9 collective-permute-start.10
  332.9 1.9 collective-permute-start.11
  336.9 5.4 all-to-all-done.3
  343.3 8.6 %collective-permute-done.8 = bf16[2,128,2048]{2,1,0:T(8,128)(2,1)} collective-permute-done((bf16[2,128,2048]{2,1,0:T(8,128)(2,1)}, bf16[2,128,2048]{2,1,0:T(8,128)(2,1)}, u32[]{:S(2)}, u32[]{:S(2)}) %collective-permute-start.8) | collective-permute-done | bytes 1048608 | tf_op jit(solution)/shard_map/ppermute | solution.py:14
  353.3 4.4 collective-permute-start.14
  359.0 34.9 %collective-permute-done.10 = bf16[2,128,2048]{2,1,0:T(8,128)(2,1)} collective-permute-done((bf16[2,128,2048]{2,1,0:T(8,128)(2,1)}, bf16[2,128,2048]{2,1,0:T(8,128)(2,1)}, u32[]{:S(2)}, u32[]{:S(2)}) %collective-permute-start.10) | collective-permute-done | bytes 1048608 | tf_op jit(solution)/shard_map/ppermute | solution.py:14
  393.9 92.4 %collective-permute-start.15 = (bf16[2,128,2048]{2,1,0:T(8,128)(2,1)S(1)}, bf16[2,128,2048]{2,1,0:T(8,128)(2,1)S(1)}, u32[]{:S(2)}, u32[]{:S(2)}) collective-permute-start(bf16[2,128,2048]{2,1,0:T(8,128)(2,1)S(1)} %get-tuple-element.29), channel_id=1, source_target_pairs={{0,2},{2,4},{4,6},{6,8},{8,10},{10,12},{12,14},{14,16},{16,18},{18... | collective-permute-start | bytes 3145736 | tf_op jit(solution)/shard_map/ppermute | solution.py:14
  490.5 19.3 %collective-permute-done.15 = bf16[2,128,2048]{2,1,0:T(8,128)(2,1)S(1)} collective-permute-done((bf16[2,128,2048]{2,1,0:T(8,128)(2,1)S(1)}, bf16[2,128,2048]{2,1,0:T(8,128)(2,1)S(1)}, u32[]{:S(2)}, u32[]{:S(2)}) %collective-permute-start.15) | collective-permute-done | bytes 1048608 | tf_op jit(solution)/shard_map/ppermute | solution.py:14
  509.9 24.9 %copy.202 = bf16[2,1024,2048]{2,0,1:T(2,128)(2,1)} copy(bf16[2,1024,2048]{2,1,0:T(8,128)(2,1)S(1)} %bitcast.171) | data formatting | bytes 16777216 | tf_op jit(solution)/shard_map/reshape | solution.py:161
  534.8 30.2 %gather_fusion.2 = bf16[768,2,2048]{2,1,0:T(2,128)(2,1)} fusion(bf16[2,1024,2048]{2,0,1:T(2,128)(2,1)} %copy.202, s32[1024]{0:T(1024)S(1)} %pad_clamp_fusion), kind=kCustom, calls=%fused_computation.4 | custom fusion | bytes 12585984 | tf_op jit(solution)/shard_map/jit(_take)/gather | solution.py:162
  565.1 9.3 %fusion.1 = bf16[2,768,2048]{2,0,1:T(2,128)(2,1)S(1)} fusion(bf16[768,2,2048]{2,1,0:T(2,128)(2,1)} %gather_fusion.2, pred[768]{0:T(1024)(128)(4,1)S(1)} %compare_and_fusion), kind=kLoop, calls=%fused_computation.23 | loop fusion | flops 3145728 | bytes 12583680 | tf_op jit(solution)/shard_map/jit(_take)/select_n | solution.py:162
  574.4 5.6 copy.203
  (116 shorter events, 34.8 us)
Async XLA Ops:
  74.3 13.1 %copy-start.6 = (bf16[128,4096]{1,0:T(8,128)(2,1)S(1)}, bf16[128,4096]{1,0:T(8,128)(2,1)}, u32[]{:S(2)}) copy-start(bf16[128,4096]{1,0:T(8,128)(2,1)} %param.10) | copy-start | bytes 3145732
  80.4 11.8 %copy-start.9 = (s32[16,8]{0,1:T(8,128)S(1)}, s32[16,8]{0,1:T(8,128)}, u32[]{:S(2)}) copy-start(s32[16,8]{0,1:T(8,128)} %param.11) | copy-start | bytes 1540
  80.4 11.9 %copy-start.8 = (s32[16,8]{0,1:T(8,128)S(1)}, s32[16,8]{0,1:T(8,128)}, u32[]{:S(2)}) copy-start(s32[16,8]{0,1:T(8,128)} %param.13) | copy-start | bytes 1540
  80.4 12.2 %copy-start.7 = (bf16[128,4096]{1,0:T(8,128)(2,1)S(1)}, bf16[128,4096]{1,0:T(8,128)(2,1)}, u32[]{:S(2)}) copy-start(bf16[128,4096]{1,0:T(8,128)(2,1)} %param.9) | copy-start | bytes 3145732
  80.5 75.9 %collective-permute-start = (bf16[2,128,2048]{1,2,0:T(8,128)(2,1)}, bf16[2,128,2048]{1,2,0:T(8,128)(2,1)}, u32[]{:S(2)}, u32[]{:S(2)}) collective-permute-start(bf16[2,128,2048]{1,2,0:T(8,128)(2,1)} %get-tuple-element.46), channel_id=1, source_target_pairs={{0,2},{2,4},{4,6},{6,8},{8,10},{10,12},{12,14},{14,16},{16,18},{18... | collective-permute-start | bytes 3145736 | tf_op jit(solution)/shard_map/ppermute | solution.py:14
  82.1 75.6 %collective-permute-start.1 = (bf16[2,128,2048]{1,2,0:T(8,128)(2,1)}, bf16[2,128,2048]{1,2,0:T(8,128)(2,1)}, u32[]{:S(2)}, u32[]{:S(2)}) collective-permute-start(bf16[2,128,2048]{1,2,0:T(8,128)(2,1)} %get-tuple-element.45), channel_id=1, source_target_pairs={{0,6},{2,8},{4,10},{6,12},{8,14},{10,16},{12,18},{14,20},{16,22},{... | collective-permute-start | bytes 3145736 | tf_op jit(solution)/shard_map/ppermute | solution.py:14
  82.2 156.3 %collective-permute-start.2 = (bf16[2,128,2048]{1,2,0:T(8,128)(2,1)}, bf16[2,128,2048]{1,2,0:T(8,128)(2,1)}, u32[]{:S(2)}, u32[]{:S(2)}) collective-permute-start(bf16[2,128,2048]{1,2,0:T(8,128)(2,1)} %get-tuple-element.44), channel_id=1, source_target_pairs={{0,10},{2,12},{4,14},{6,16},{8,18},{10,20},{12,22},{14,24},{16,26}... | collective-permute-start | bytes 3145736 | tf_op jit(solution)/shard_map/ppermute | solution.py:14
  84.7 176.2 %collective-permute-start.3 = (bf16[2,128,2048]{1,2,0:T(8,128)(2,1)}, bf16[2,128,2048]{1,2,0:T(8,128)(2,1)}, u32[]{:S(2)}, u32[]{:S(2)}) collective-permute-start(bf16[2,128,2048]{1,2,0:T(8,128)(2,1)} %get-tuple-element.43), channel_id=1, source_target_pairs={{0,14},{2,16},{4,18},{6,20},{8,22},{10,24},{12,26},{14,28},{16,30}... | collective-permute-start | bytes 3145736 | tf_op jit(solution)/shard_map/ppermute | solution.py:14
  84.8 177.5 %collective-permute-start.4 = (bf16[2,128,2048]{1,2,0:T(8,128)(2,1)}, bf16[2,128,2048]{1,2,0:T(8,128)(2,1)}, u32[]{:S(2)}, u32[]{:S(2)}) collective-permute-start(bf16[2,128,2048]{1,2,0:T(8,128)(2,1)} %get-tuple-element.42), channel_id=1, source_target_pairs={{0,18},{2,20},{4,22},{6,24},{8,26},{10,28},{12,30},{14,0},{16,2},{... | collective-permute-start | bytes 3145736 | tf_op jit(solution)/shard_map/ppermute | solution.py:14
  88.7 15.8 %all-to-all-start.1 = ((bf16[128,2,2048]{0,2,1:T(8,128)(2,1)}), bf16[128,2,2048]{0,2,1:T(8,128)(2,1)S(1)}, u32[]{:S(2)}, u32[]{:S(2)}) async-start(bf16[128,2,2048]{0,2,1:T(8,128)(2,1)} %bitcast.33), calls=%async_computation.1 | async-start | bytes 2097152 | tf_op jit(solution)/shard_map/all_to_all | solution.py:101
  104.5 17.6 %all-to-all-start = ((bf16[128,2,2048]{0,2,1:T(8,128)(2,1)}), bf16[128,2,2048]{0,2,1:T(8,128)(2,1)S(1)}, u32[]{:S(2)}, u32[]{:S(2)}) async-start(bf16[128,2,2048]{0,2,1:T(8,128)(2,1)} %bitcast.30), calls=%async_computation | async-start | bytes 2097152 | tf_op jit(solution)/shard_map/all_to_all | solution.py:100
  122.5 1.6 copy-start
  155.1 1.3 copy-start.4
  155.7 2.0 copy-start.3
  155.7 82.7 %copy-start.2 = (bf16[2,128,2048]{1,2,0:T(8,128)(2,1)S(1)}, bf16[2,128,2048]{1,2,0:T(8,128)(2,1)}, u32[]{:S(2)}) copy-start(bf16[2,128,2048]{1,2,0:T(8,128)(2,1)} %get-tuple-element.39) | copy-start | bytes 3145732
  156.4 107.3 %collective-permute-start.5 = (bf16[2,128,2048]{1,2,0:T(8,128)(2,1)S(1)}, bf16[2,128,2048]{1,2,0:T(8,128)(2,1)S(1)}, u32[]{:S(2)}, u32[]{:S(2)}) collective-permute-start(bf16[2,128,2048]{1,2,0:T(8,128)(2,1)S(1)} %copy-done.4), channel_id=1, source_target_pairs={{0,22},{2,24},{4,26},{6,28},{8,30},{10,0},{12,2},{14,4},{16,6},{18... | collective-permute-start | bytes 3145736 | tf_op jit(solution)/shard_map/ppermute | solution.py:14
  157.8 106.8 %collective-permute-start.6 = (bf16[2,128,2048]{1,2,0:T(8,128)(2,1)S(1)}, bf16[2,128,2048]{1,2,0:T(8,128)(2,1)S(1)}, u32[]{:S(2)}, u32[]{:S(2)}) collective-permute-start(bf16[2,128,2048]{1,2,0:T(8,128)(2,1)S(1)} %copy-done.3), channel_id=1, source_target_pairs={{0,26},{2,28},{4,30},{6,0},{8,2},{10,4},{12,6},{14,8},{16,10},{18,... | collective-permute-start | bytes 3145736 | tf_op jit(solution)/shard_map/ppermute | solution.py:14
  238.5 27.1 %collective-permute-start.7 = (bf16[2,128,2048]{1,2,0:T(8,128)(2,1)S(1)}, bf16[2,128,2048]{1,2,0:T(8,128)(2,1)S(1)}, u32[]{:S(2)}, u32[]{:S(2)}) collective-permute-start(bf16[2,128,2048]{1,2,0:T(8,128)(2,1)S(1)} %copy-done.2), channel_id=1, source_target_pairs={{0,30},{2,0},{4,2},{6,4},{8,6},{10,8},{12,10},{14,12},{16,14},{18,... | collective-permute-start | bytes 3145736 | tf_op jit(solution)/shard_map/ppermute | solution.py:14
  290.4 1.9 copy-start.1
  302.8 23.5 %all-to-all-start.2 = ((bf16[2,128,2048]{2,1,0:T(8,128)(2,1)}), bf16[2,128,2048]{2,1,0:T(8,128)(2,1)S(1)}, u32[]{:S(2)}, u32[]{:S(2)}) async-start(bf16[2,128,2048]{2,1,0:T(8,128)(2,1)} %bitcast.41), calls=%async_computation.2 | async-start | bytes 2097152 | tf_op jit(solution)/shard_map/all_to_all | solution.py:166
  325.2 26.7 %collective-permute-start.8 = (bf16[2,128,2048]{2,1,0:T(8,128)(2,1)}, bf16[2,128,2048]{2,1,0:T(8,128)(2,1)}, u32[]{:S(2)}, u32[]{:S(2)}) collective-permute-start(bf16[2,128,2048]{2,1,0:T(8,128)(2,1)} %get-tuple-element.30), channel_id=1, source_target_pairs={{0,30},{2,0},{4,2},{6,4},{8,6},{10,8},{12,10},{14,12},{16,14},{18,... | collective-permute-start | bytes 3145736 | tf_op jit(solution)/shard_map/ppermute | solution.py:14
  326.2 27.0 %collective-permute-start.9 = (bf16[2,128,2048]{2,1,0:T(8,128)(2,1)}, bf16[2,128,2048]{2,1,0:T(8,128)(2,1)}, u32[]{:S(2)}, u32[]{:S(2)}) collective-permute-start(bf16[2,128,2048]{2,1,0:T(8,128)(2,1)} %get-tuple-element.31), channel_id=1, source_target_pairs={{0,26},{2,28},{4,30},{6,0},{8,2},{10,4},{12,6},{14,8},{16,10},{18,... | collective-permute-start | bytes 3145736 | tf_op jit(solution)/shard_map/ppermute | solution.py:14
  326.3 15.9 %all-to-all-start.3 = ((bf16[2,128,2048]{2,1,0:T(8,128)(2,1)}), bf16[2,128,2048]{2,1,0:T(8,128)(2,1)S(1)}, u32[]{:S(2)}, u32[]{:S(2)}) async-start(bf16[2,128,2048]{2,1,0:T(8,128)(2,1)} %bitcast.44), calls=%async_computation.3 | async-start | bytes 2097152 | tf_op jit(solution)/shard_map/all_to_all | solution.py:167
  330.0 64.0 %collective-permute-start.10 = (bf16[2,128,2048]{2,1,0:T(8,128)(2,1)}, bf16[2,128,2048]{2,1,0:T(8,128)(2,1)}, u32[]{:S(2)}, u32[]{:S(2)}) collective-permute-start(bf16[2,128,2048]{2,1,0:T(8,128)(2,1)} %get-tuple-element.32), channel_id=1, source_target_pairs={{0,22},{2,24},{4,26},{6,28},{8,30},{10,0},{12,2},{14,4},{16,6},{18... | collective-permute-start | bytes 3145736 | tf_op jit(solution)/shard_map/ppermute | solution.py:14
  332.9 154.7 %collective-permute-start.11 = (bf16[2,128,2048]{2,1,0:T(8,128)(2,1)}, bf16[2,128,2048]{2,1,0:T(8,128)(2,1)}, u32[]{:S(2)}, u32[]{:S(2)}) collective-permute-start(bf16[2,128,2048]{2,1,0:T(8,128)(2,1)} %get-tuple-element.33), channel_id=1, source_target_pairs={{0,18},{2,20},{4,22},{6,24},{8,26},{10,28},{12,30},{14,0},{16,2},{... | collective-permute-start | bytes 3145736 | tf_op jit(solution)/shard_map/ppermute | solution.py:14
  334.8 154.2 %collective-permute-start.12 = (bf16[2,128,2048]{2,1,0:T(8,128)(2,1)}, bf16[2,128,2048]{2,1,0:T(8,128)(2,1)}, u32[]{:S(2)}, u32[]{:S(2)}) collective-permute-start(bf16[2,128,2048]{2,1,0:T(8,128)(2,1)} %get-tuple-element.34), channel_id=1, source_target_pairs={{0,14},{2,16},{4,18},{6,20},{8,22},{10,24},{12,26},{14,28},{16,30}... | collective-permute-start | bytes 3145736 | tf_op jit(solution)/shard_map/ppermute | solution.py:14
  336.9 16.4 %copy-start.5 = (bf16[2,128,2048]{2,1,0:T(8,128)(2,1)S(1)}, bf16[2,128,2048]{2,1,0:T(8,128)(2,1)}, u32[]{:S(2)}) copy-start(bf16[2,128,2048]{2,1,0:T(8,128)(2,1)} %get-tuple-element.36) | copy-start | bytes 3145732
  351.9 138.4 %collective-permute-start.13 = (bf16[2,128,2048]{2,1,0:T(8,128)(2,1)}, bf16[2,128,2048]{2,1,0:T(8,128)(2,1)S(1)}, u32[]{:S(2)}, u32[]{:S(2)}) collective-permute-start(bf16[2,128,2048]{2,1,0:T(8,128)(2,1)} %get-tuple-element.35), channel_id=1, source_target_pairs={{0,10},{2,12},{4,14},{6,16},{8,18},{10,20},{12,22},{14,24},{16,26}... | collective-permute-start | bytes 3145736 | tf_op jit(solution)/shard_map/ppermute | solution.py:14
  353.3 137.1 %collective-permute-start.14 = (bf16[2,128,2048]{2,1,0:T(8,128)(2,1)S(1)}, bf16[2,128,2048]{2,1,0:T(8,128)(2,1)S(1)}, u32[]{:S(2)}, u32[]{:S(2)}) collective-permute-start(bf16[2,128,2048]{2,1,0:T(8,128)(2,1)S(1)} %copy-done.5), channel_id=1, source_target_pairs={{0,6},{2,8},{4,10},{6,12},{8,14},{10,16},{12,18},{14,20},{16,22},{... | collective-permute-start | bytes 3145736 | tf_op jit(solution)/shard_map/ppermute | solution.py:14
  393.9 115.9 %collective-permute-start.15 = (bf16[2,128,2048]{2,1,0:T(8,128)(2,1)S(1)}, bf16[2,128,2048]{2,1,0:T(8,128)(2,1)S(1)}, u32[]{:S(2)}, u32[]{:S(2)}) collective-permute-start(bf16[2,128,2048]{2,1,0:T(8,128)(2,1)S(1)} %get-tuple-element.29), channel_id=1, source_target_pairs={{0,2},{2,4},{4,6},{6,8},{8,10},{10,12},{12,14},{14,16},{16,18},{18... | collective-permute-start | bytes 3145736 | tf_op jit(solution)/shard_map/ppermute | solution.py:14
where the time goes:
time: 592 us; the launch traced here: 580 us
  local copies, waits for them, and re-layouts  200 us (34%)
  waiting for transfers between devices  184 us (31%)
  starting transfers between devices  130 us (22%)
  other arithmetic  45.4 us (8%)
  matrix products  18.6 us (3%)
    ppermute x16, waiting for transfers between devices, from_behind(): lax.ppermute(shard, axis, [(i, (i + by) % devices) for i in range(devices)])  162 us
    ppermute x16, starting transfers between devices, from_behind(): lax.ppermute(shard, axis, [(i, (i + by) % devices) for i in range(devices)])  114 us
    gather x2, local copies, waits for them, and re-layouts, body(): jnp.take(memory, key_index.reshape(-1), axis=1)  62.8 us
    gather x1, local copies, waits for them, and re-layouts, body(): memory_grad = jnp.take(back, enc_token, axis=1)  30.2 us
    unnamed x42, local copies, waits for them, and re-layouts  25.8 us
    reshape x1, local copies, waits for them, and re-layouts, body(): back = jnp.stack(returned, axis=1).reshape(2, examples * ENC_MAX, width)  24.9 us
    gather x1, local copies, waits for them, and re-layouts, body(): jnp.take(paired, dec_index.reshape(-1), axis=1)  18.5 us
    another operation x2, local copies, waits for them, and re-layouts, body(): outgoing = jnp.stack([key_grad, value_grad])  12.9 us
  transfers between devices with their start and end apart: 20, of which 10 were waited for; matrix products, arithmetic and copies ran while one was open for 13% of the time, Pallas kernels for 0%

commit v1 on v0

v1 whole, which is shorter than its diff:
```python
import functools

import jax
import jax.numpy as jnp
from jax import lax
from jax.experimental import pallas as pl
from jax.experimental.pallas import tpu as pltpu
from jax.sharding import PartitionSpec as P

HD = 128
ENC_MAX = 128
DEC_MAX = 64
PARTNERS = 8
CHUNKS = 4
BF16 = jnp.bfloat16
F32 = jnp.float32
MESH = pl.DeviceIdType.MESH


def matmul(a, b, dims):
    return lax.dot_general(a, b, (dims, ((), ())), preferred_element_type=F32)


NN = ((1,), (0,))
NT = ((1,), (1,))
TN = ((0,), (0,))


def kernel(
    sections,
    tensors,
    mem_hbm,
    q_hbm,
    g_hbm,
    enc_len,
    dec_len,
    readers,
    att_hbm,
    qg_hbm,
    mg_hbm,
    mem_v,
    dec_v,
    fsend,
    frecv,
    osend,
    oret,
    fin_v,
    kv_x,
    d_x,
    pack_m,
    unpack_m,
    enc_m,
    grad_m,
    meta,
    a_send,
    a_recv,
    a_local,
    f_send,
    f_recv,
    o_send,
    o_recv,
    g_send,
    g_recv,
    g_local,
    m_in,
    m_out,
):
    me = lax.axis_index("section")
    mine = lax.axis_index("tensor")
    rows = q_hbm.shape[0]
    enc_count = mem_v.shape[1]
    dec_count = dec_v.shape[2]
    width = mem_v.shape[2]
    piece = width // CHUNKS
    spacing = sections // PARTNERS
    scaling = HD ** (-0.5)

    def holder_of(slot):
        return lax.rem(me + 2 * sections - slot * spacing - 1, sections)

    def reader_of(slot):
        return lax.rem(me + slot * spacing + 1, sections)

    def peer_of(step):
        return lax.rem(mine + step, tensors)

    mem_copy = pltpu.make_async_copy(mem_hbm, mem_v, m_in)
    mem_copy.start()

    barrier = pltpu.get_barrier_semaphore()
    for step in range(1, tensors):
        pl.semaphore_signal(
            barrier, inc=1, device_id={"tensor": peer_of(step)}, device_id_type=MESH
        )
    for slot in range(PARTNERS):
        pl.semaphore_signal(
            barrier, inc=1, device_id={"section": holder_of(slot)}, device_id_type=MESH
        )
        pl.semaphore_signal(
            barrier, inc=1, device_id={"section": reader_of(slot)}, device_id_type=MESH
        )
    pl.semaphore_wait(barrier, tensors - 1 + 2 * PARTNERS)

    own_rows = pl.ds(pl.multiple_of(mine * rows, rows), rows)

    def first_copy(c, a, step):
        peer = peer_of(step)
        source = (q_hbm, g_hbm)[a]
        columns = pl.ds(pl.multiple_of(peer * width + c * piece, piece), piece)
        if step == 0:
            return pltpu.make_async_copy(
                source.at[:, columns], dec_v.at[c, a, own_rows], a_local.at[c, a]
            )
        return pltpu.make_async_remote_copy(
            src_ref=source.at[:, columns],
            dst_ref=dec_v.at[c, a, own_rows],
            send_sem=a_send.at[c, a, step - 1],
            recv_sem=a_recv.at[c, a, step - 1],
            device_id={"tensor": peer},
            device_id_type=MESH,
        )

    for c in range(CHUNKS):
        for a in range(2):
            for step in list(range(1, tensors)) + [0]:
                first_copy(c, a, step).start()

    start = jnp.int32(0)
    for i in range(PARTNERS):
        length = dec_len[me, i]
        meta[0, i] = start
        meta[1, i] = length
        start = start + length
    for slot in range(PARTNERS):
        reader = reader_of(slot)
        start, begin, size = jnp.int32(0), jnp.int32(0), jnp.int32(0)
        for j in range(PARTNERS):
            length = enc_len[me, j]
            match = readers[me, j] == reader
            begin = jnp.where(match, start, begin)
            size = jnp.where(match, length, size)
            start = start + length
        meta[2, slot] = begin
        meta[3, slot] = size

    def one_hot(hits):
        return jnp.where(hits, 1.0, 0.0).astype(BF16)

    def iota(shape, dim):
        return lax.broadcasted_iota(jnp.int32, shape, dim)

    half = PARTNERS // 2
    for i in range(PARTNERS):
        shape = (DEC_MAX, dec_count)
        within = iota(shape, 0)
        hits = (iota(shape, 1) - within == meta[0, i]) & (within < meta[1, i])
        pack_m[i // half, (i % half) * DEC_MAX : (i % half + 1) * DEC_MAX, :] = one_hot(hits)

    def forward_copy(c, slot):
        holder = holder_of(slot)
        return pltpu.make_async_remote_copy(
            src_ref=fsend.at[c, :, lax.div(holder, spacing)],
            dst_ref=frecv.at[c, :, slot],
            send_sem=f_send.at[c, slot],
            recv_sem=f_recv.at[c, slot],
            device_id={"section": holder},
            device_id_type=MESH,
        )

    def back_copy(c, slot):
        return pltpu.make_async_remote_copy(
            src_ref=osend.at[c, :, slot],
            dst_ref=oret.at[c, :, lax.div(me, spacing)],
            send_sem=o_send.at[c, slot],
            recv_sem=o_recv.at[c, lax.div(me, spacing)],
            device_id={"section": reader_of(slot)},
            device_id_type=MESH,
        )

    def back_arrival(c, i):
        return pltpu.make_async_remote_copy(
            src_ref=osend.at[c, :, i],
            dst_ref=oret.at[c, :, i],
            send_sem=o_send.at[c, i],
            recv_sem=o_recv.at[c, i],
            device_id={"section": reader_of(i)},
            device_id_type=MESH,
        )

    def last_copy(c, a, step):
        peer = peer_of(step)
        target = (att_hbm, qg_hbm)[a]
        source = fin_v.at[c, a, pl.ds(pl.multiple_of(peer * rows, rows), rows)]
        columns = pl.ds(pl.multiple_of(mine * width + c * piece, piece), piece)
        if step == 0:
            return pltpu.make_async_copy(source, target.at[:, columns], g_local.at[c, a])
        return pltpu.make_async_remote_copy(
            src_ref=source,
            dst_ref=target.at[:, columns],
            send_sem=g_send.at[c, a, step - 1],
            recv_sem=g_recv.at[c, a, step - 1],
            device_id={"tensor": peer},
            device_id_type=MESH,
        )

    def grad_copy(c):
        columns = pl.ds(c * piece, piece)
        return pltpu.make_async_copy(
            mem_v.at[:, :, columns], mg_hbm.at[:, :, columns], m_out.at[c]
        )

    def pack(c):
        for a in range(2):
            first_copy(c, a, 0).wait()
            for step in range(1, tensors):
                first_copy(c, a, step).wait_recv()
        for a in range(2):
            for g in range(2):
                block = matmul(pack_m[g], dec_v[c, a], NN).astype(BF16)
                fsend[c, a, g * half : (g + 1) * half] = block.reshape(half, DEC_MAX, piece)

        @pl.loop(0, PARTNERS)
        def _(slot):
            forward_copy(c, slot).start()

    def expand(c):
        @pl.loop(0, PARTNERS // 2)
        def _(g):
            for a in range(2):
                block = matmul(enc_m[g], mem_v[a, :, c * piece : (c + 1) * piece], NN)
                kv_x[c, a, pl.ds(g * 2, 2)] = block.astype(BF16).reshape(2, ENC_MAX, piece)

    def attend(c):
        @pl.loop(0, PARTNERS)
        def _(slot):
            forward_copy(c, slot).wait_recv()
            valid = iota((DEC_MAX, ENC_MAX), 1) < meta[3, slot]
            for h in range(piece // HD):
                at = slice(h * HD, (h + 1) * HD)
                q = frecv[c, 0, slot, :, at]
                g = frecv[c, 1, slot, :, at]
                k = kv_x[c, 0, slot, :, at]
                v = kv_x[c, 1, slot, :, at]
                scores = jnp.where(valid, matmul(q, k, NT) * scaling, -jnp.inf)
                weights = jnp.exp(scores - jnp.max(scores, axis=1, keepdims=True))
                probs = weights / jnp.sum(weights, axis=1, keepdims=True)
                low = probs.astype(BF16)
                dprobs = matmul(g, v, NT)
                delta = jnp.sum(probs * dprobs, axis=1, keepdims=True)
                dscores = (probs * (dprobs - delta)).astype(BF16)
                osend[c, 0, slot, :, at] = matmul(low, v, NN).astype(BF16)
                osend[c, 1, slot, :, at] = (matmul(dscores, k, NN) * scaling).astype(BF16)
                d_x[0, slot, :, at] = (matmul(dscores, q, TN) * scaling).astype(BF16)
                d_x[1, slot, :, at] = matmul(low, g, TN).astype(BF16)
            back_copy(c, slot).start()

    def collect(c):
        @pl.loop(0, enc_count // 256)
        def _(b):
            at = pl.ds(pl.multiple_of(b * 256, 256), 256)
            for a in range(2):
                block = d_x[a].reshape(PARTNERS * ENC_MAX, piece)
                mem_v[a, at, c * piece : (c + 1) * piece] = matmul(
                    grad_m[at, :], block, NN
                ).astype(BF16)

        grad_copy(c).start()

    def finish(c):
        @pl.loop(0, PARTNERS)
        def _(i):
            back_arrival(c, i).wait_recv()

        for a in range(2):
            block = oret[c, a].reshape(PARTNERS * DEC_MAX, piece)
            fin_v[c, a] = matmul(unpack_m[...], block, NN).astype(BF16)
            for step in list(range(1, tensors)) + [0]:
                last_copy(c, a, step).start()

    pack(0)

    for slot in range(PARTNERS):
        shape = (ENC_MAX, enc_count)
        within = iota(shape, 0)
        hits = (iota(shape, 1) - within == meta[2, slot]) & (within < meta[3, slot])
        enc_m[slot // 2, (slot % 2) * ENC_MAX : (slot % 2 + 1) * ENC_MAX, :] = one_hot(hits)
    mem_copy.wait()
    expand(0)
    pack(1)

    position = iota((dec_count, 1), 0)
    goal = jnp.full((dec_count, 1), -1, jnp.int32)
    for i in range(PARTNERS):
        within = position - meta[0, i]
        goal = jnp.where((within >= 0) & (within < meta[1, i]), within + i * DEC_MAX, goal)
    unpack_m[...] = one_hot(iota((dec_count, PARTNERS * DEC_MAX), 1) == goal)
    for b in range(enc_count // 256):
        position = iota((256, 1), 0) + b * 256
        goal = jnp.full((256, 1), -1, jnp.int32)
        for slot in range(PARTNERS):
            within = position - meta[2, slot]
            goal = jnp.where(
                (within >= 0) & (within < meta[3, slot]), within + slot * ENC_MAX, goal
            )
        hits = iota((256, PARTNERS * ENC_MAX), 1) == goal
        grad_m[b * 256 : (b + 1) * 256, :] = one_hot(hits)

    expand(1)
    for c in range(2, CHUNKS):
        pack(c)
        expand(c)
    for c in range(CHUNKS):
        attend(c)
        collect(c)
        if c:
            finish(c - 1)
    finish(CHUNKS - 1)

    for c in range(CHUNKS):
        for a in range(2):
            for step in range(1, tensors):
                first_copy(c, a, step).wait_send()
                last_copy(c, a, step).wait()
            last_copy(c, a, 0).wait()
        grad_copy(c).wait()

        @pl.loop(0, PARTNERS)
        def _(slot):
            forward_copy(c, slot).wait_send()
            back_copy(c, slot).wait_send()


def body(sections, tensors, memory, queries, out_grad, enc_lengths, dec_lengths, readers):
    enc_count, width = memory.shape[1:]
    rows = queries.shape[0]
    dec_count = rows * tensors
    piece = width // CHUNKS
    blocks = (CHUNKS, 2, PARTNERS, DEC_MAX, piece)
    peers = max(tensors - 1, 1)
    anywhere = pl.BlockSpec(memory_space=pl.ANY)
    scalars = pl.BlockSpec(memory_space=pltpu.SMEM)
    dma = pltpu.SemaphoreType.DMA
    return pl.pallas_call(
        functools.partial(kernel, sections, tensors),
        out_shape=(
            jax.ShapeDtypeStruct(queries.shape, BF16),
            jax.ShapeDtypeStruct(queries.shape, BF16),
            jax.ShapeDtypeStruct(memory.shape, BF16),
        ),
        in_specs=[anywhere] * 3 + [scalars] * 3,
        out_specs=(anywhere,) * 3,
        scratch_shapes=[
            pltpu.VMEM((2, enc_count, width), BF16),
            pltpu.VMEM((CHUNKS, 2, dec_count, piece), BF16),
            pltpu.VMEM(blocks, BF16),
            pltpu.VMEM(blocks, BF16),
            pltpu.VMEM(blocks, BF16),
            pltpu.VMEM(blocks, BF16),
            pltpu.VMEM((CHUNKS, 2, dec_count, piece), BF16),
            pltpu.VMEM((CHUNKS, 2, PARTNERS, ENC_MAX, piece), BF16),
            pltpu.VMEM((2, PARTNERS, ENC_MAX, piece), BF16),
            pltpu.VMEM((2, PARTNERS // 2 * DEC_MAX, dec_count), BF16),
            pltpu.VMEM((dec_count, PARTNERS * DEC_MAX), BF16),
            pltpu.VMEM((PARTNERS // 2, 2 * ENC_MAX, enc_count), BF16),
            pltpu.VMEM((enc_count, PARTNERS * ENC_MAX), BF16),
            pltpu.SMEM((4, PARTNERS), jnp.int32),
            dma((CHUNKS, 2, peers)),
            dma((CHUNKS, 2, peers)),
            dma((CHUNKS, 2)),
            dma((CHUNKS, PARTNERS)),
            dma((CHUNKS, PARTNERS)),
            dma((CHUNKS, PARTNERS)),
            dma((CHUNKS, PARTNERS)),
            dma((CHUNKS, 2, peers)),
            dma((CHUNKS, 2, peers)),
            dma((CHUNKS, 2)),
            dma,
            dma((CHUNKS,)),
        ],
        compiler_params=pltpu.CompilerParams(
            collective_id=0, has_side_effects=True, vmem_limit_bytes=60 * 1024 * 1024
        ),
    )(memory, queries, out_grad, enc_lengths, dec_lengths, readers)


def solution(mesh):
    placed = (
        P(None, "section", "tensor"),
        P(("section", "tensor"), None),
        P(("section", "tensor"), None),
        P(),
        P(),
        P(),
    )
    return jax.shard_map(
        functools.partial(body, mesh.shape["section"], mesh.shape["tensor"]),
        mesh=mesh,
        in_specs=placed,
        out_specs=(
            P(("section", "tensor"), None),
            P(("section", "tensor"), None),
            P(None, "section", "tensor"),
        ),
        check_vma=False,
    )
```

time: 592 us -> 220 us (0.37); the launches traced: 580 us -> 220 us
  Pallas kernels: 0 us -> 204 us
  local copies, waits for them, and re-layouts: 200 us -> 15.3 us
  waiting for transfers between devices: 184 us -> 0 us
  starting transfers between devices: 130 us -> 0 us
  other arithmetic: 45.4 us -> 0 us
  matrix products: 18.6 us -> 0 us
    pallas_call x0 -> x1, Pallas kernels: none -> 204 us  [body(): pl.pallas_call(functools.partial(kernel, sections, tensors), out_shape=(j...]
    ppermute x16 -> x0, waiting for transfers between devices: 162 us -> none  [from_behind(): lax.ppermute(shard, axis, [(i, (i + by) % devices) for i in range(devices)])]
    gather x6 -> x0, local copies, waits for them, and re-layouts: 117 us -> none  [the longest x2 62.8 us: body(): jnp.take(memory, key_index.reshape(-1), axis=1)]
    ppermute x16 -> x0, starting transfers between devices: 114 us -> none  [from_behind(): lax.ppermute(shard, axis, [(i, (i + by) % devices) for i in range(devices)])]
    select_n x9 -> x0, other arithmetic: 25.6 us -> none  [the longest x2 9.33 us: body(): memory_grad = jnp.take(back, enc_token, axis=1)]
    reshape x3 -> x0, local copies, waits for them, and re-layouts: 25.1 us -> none  [the longest x1 24.9 us: body(): back = jnp.stack(returned, axis=1).reshape(2, examples * ENC_MAX, width)]
    all_to_all x4 -> x0, waiting for transfers between devices: 22.5 us -> none  [the longest x1 8.79 us: body(): lax.all_to_all(out_grad, 'tensor', split_axis=1, concat_axis=0, tiled=True)]
    dot_general x6 -> x0, matrix products: 18.6 us -> none  [the longest x1 4.16 us: attend(): jnp.einsum('ehqk,ekhd->eqhd', probs_low, value_heads, preferred_element_t...]
  transfers between devices with their start and end apart: 20 -> 0, of which waited for: 10 -> 0; matrix products, arithmetic and copies ran while one was open for 13% -> 0% of each run, Pallas kernels for 0% -> 0%
where the time goes in v1:
time: 220 us
  Pallas kernels  204 us (93%)
  local copies, waits for them, and re-layouts  15.3 us (7%)
    pallas_call x1, Pallas kernels, body(): pl.pallas_call(functools.partial(kernel, sections, tensors), out_shape=(j...  204 us
    unnamed x6, local copies, waits for them, and re-layouts  15.3 us

profile of v1, /device:TPU:15, one launch (start us, length us, event | category | flops | bytes accessed | tf_op | source)
XLA Modules:
  0.0 220.0 jit_solution(1742242312808253769)
XLA Ops:
  0.6 1.4 copy.9.enc_len
  2.0 1.4 copy.10.dec_len
  3.3 1.4 copy.11.readers
  4.7 204.1 %shard_map.85 = (bf16[128,4096]{1,0:T(8,128)(2,1)}, bf16[128,4096]{1,0:T(8,128)(2,1)}, bf16[2,768,2048]{2,1,0:T(8,128)(2,1)}) custom-call(bf16[2,768,2048]{2,1,0:T(8,128)(2,1)} %mem_hbm.1, bf16[128,4096]{1,0:T(8,128)(2,1)} %q_hbm.1, bf16[128,4096]{1,0:T(8,128)(2,1)} %g_hbm.1, s32[16,8]{1,0:T(8,128)} %copy.9.enc_len, s32[16,8]{1,0:T(8,128)} %copy.10.dec_len, ...), custom_call_target="tpu_custom_call" | custom-call | tf_op jit(solution)/shard_map/pallas_call | solution.py:343
  208.8 2.3 %copy.15 = bf16[128,4096]{1,0:T(8,128)(2,1)} copy(bf16[128,4096]{1,0:T(8,128)(2,1)} %get-tuple-element.6) | data formatting | bytes 2097152
  211.1 2.3 %copy.16 = bf16[128,4096]{1,0:T(8,128)(2,1)} copy(bf16[128,4096]{1,0:T(8,128)(2,1)} %get-tuple-element.7) | data formatting | bytes 2097152
  213.4 6.6 %copy.17 = bf16[2,768,2048]{2,1,0:T(8,128)(2,1)} copy(bf16[2,768,2048]{2,1,0:T(8,128)(2,1)} %get-tuple-element.8) | data formatting | bytes 12582912

commit v2 on v1

--- a/solution.py
+++ b/solution.py
@@ -11,7 +11,7 @@
 ENC_MAX = 128
 DEC_MAX = 64
 PARTNERS = 8
-CHUNKS = 4
+MOST_CHUNKS = 8
 BF16 = jnp.bfloat16
 F32 = jnp.float32
 MESH = pl.DeviceIdType.MESH
@@ -24,6 +24,10 @@
 NN = ((1,), (0,))
 NT = ((1,), (1,))
 TN = ((0,), (0,))
+
+
+def chunk_count(width):
+    return min(MOST_CHUNKS, width // HD)
 
 
 def kernel(
@@ -32,12 +36,12 @@
     mem_hbm,
     q_hbm,
     g_hbm,
-    enc_len,
-    dec_len,
-    readers,
-    att_hbm,
-    qg_hbm,
-    mg_hbm,
+    enc_hbm,
+    dec_hbm,
+    readers_hbm,
+    att_out,
+    qg_out,
+    mg_out,
     mem_v,
     dec_v,
     fsend,
@@ -51,6 +55,9 @@
     unpack_m,
     enc_m,
     grad_m,
+    enc_len,
+    dec_len,
+    readers,
     meta,
     a_send,
     a_recv,
@@ -63,7 +70,7 @@
     g_recv,
     g_local,
     m_in,
-    m_out,
+    s_in,
 ):
     me = lax.axis_index("section")
     mine = lax.axis_index("tensor")
@@ -71,7 +78,8 @@
     enc_count = mem_v.shape[1]
     dec_count = dec_v.shape[2]
     width = mem_v.shape[2]
-    piece = width // CHUNKS
+    chunks = chunk_count(width)
+    piece = width // chunks
     spacing = sections // PARTNERS
     scaling = HD ** (-0.5)
 
@@ -81,11 +89,32 @@
     def reader_of(slot):
         return lax.rem(me + slot * spacing + 1, sections)
 
+    half = PARTNERS // 2
+
+    def rank_at(turn):
+        other = lax.rem(lax.div(turn, half) + 1 + lax.div(2 * me, sections), 2)
+        return other * half + lax.rem(turn + lax.div(me, spacing), half)
+
+    def holder_slot(turn):
+        holder = lax.rem(me + sections - 1, spacing) + spacing * rank_at(turn)
+        return lax.div(lax.rem(me + sections - holder - 1 + sections, sections), spacing)
+
+    def reader_slot(turn):
+        reader = lax.rem(me + 1, spacing) + spacing * rank_at(turn)
+        return lax.div(lax.rem(reader + 2 * sections - me - 1, sections), spacing)
+
     def peer_of(step):
         return lax.rem(mine + step, tensors)
 
     mem_copy = pltpu.make_async_copy(mem_hbm, mem_v, m_in)
-    mem_copy.start()
+    scalar_copies = [
+        pltpu.make_async_copy(source, target, s_in.at[i])
+        for i, (source, target) in enumerate(
+            ((enc_hbm, enc_len), (dec_hbm, dec_len), (readers_hbm, readers))
+        )
+    ]
+    for copy in scalar_copies:
+        copy.start()
 
     barrier = pltpu.get_barrier_semaphore()
     for step in range(1, tensors):
@@ -120,14 +149,19 @@
             device_id_type=MESH,
         )
 
-    for c in range(CHUNKS):
+    def fetch(c):
         for a in range(2):
             for step in list(range(1, tensors)) + [0]:
                 first_copy(c, a, step).start()
 
+    fetch(0)
+    mem_copy.start()
+    for copy in scalar_copies:
+        copy.wait()
+
     start = jnp.int32(0)
     for i in range(PARTNERS):
-        length = dec_len[me, i]
+        length = dec_len[i, me]
         meta[0, i] = start
         meta[1, i] = length
         start = start + length
@@ -135,8 +169,8 @@
         reader = reader_of(slot)
         start, begin, size = jnp.int32(0), jnp.int32(0), jnp.int32(0)
         for j in range(PARTNERS):
-            length = enc_len[me, j]
-            match = readers[me, j] == reader
+            length = enc_len[j, me]
+            match = readers[j, me] == reader
             begin = jnp.where(match, start, begin)
             size = jnp.where(match, length, size)
             start = start + length
@@ -149,7 +183,6 @@
     def iota(shape, dim):
         return lax.broadcasted_iota(jnp.int32, shape, dim)
 
-    half = PARTNERS // 2
     for i in range(PARTNERS):
         shape = (DEC_MAX, dec_count)
         within = iota(shape, 0)
@@ -189,7 +222,7 @@
 
     def last_copy(c, a, step):
         peer = peer_of(step)
-        target = (att_hbm, qg_hbm)[a]
+        target = (att_out, qg_out)[a]
         source = fin_v.at[c, a, pl.ds(pl.multiple_of(peer * rows, rows), rows)]
         columns = pl.ds(pl.multiple_of(mine * width + c * piece, piece), piece)
         if step == 0:
@@ -203,25 +236,21 @@
             device_id_type=MESH,
         )
 
-    def grad_copy(c):
-        columns = pl.ds(c * piece, piece)
-        return pltpu.make_async_copy(
-            mem_v.at[:, :, columns], mg_hbm.at[:, :, columns], m_out.at[c]
-        )
-
     def pack(c):
         for a in range(2):
             first_copy(c, a, 0).wait()
             for step in range(1, tensors):
                 first_copy(c, a, step).wait_recv()
+        if c + 1 < chunks:
+            fetch(c + 1)
         for a in range(2):
             for g in range(2):
                 block = matmul(pack_m[g], dec_v[c, a], NN).astype(BF16)
                 fsend[c, a, g * half : (g + 1) * half] = block.reshape(half, DEC_MAX, piece)
 
         @pl.loop(0, PARTNERS)
-        def _(slot):
-            forward_copy(c, slot).start()
+        def _(turn):
+            forward_copy(c, holder_slot(jnp.int32(turn))).start()
 
     def expand(c):
         @pl.loop(0, PARTNERS // 2)
@@ -232,7 +261,8 @@
 
     def attend(c):
         @pl.loop(0, PARTNERS)
-        def _(slot):
+        def _(turn):
+            slot = reader_slot(jnp.int32(turn))
             forward_copy(c, slot).wait_recv()
             valid = iota((DEC_MAX, ENC_MAX), 1) < meta[3, slot]
             for h in range(piece // HD):
@@ -260,11 +290,9 @@
             at = pl.ds(pl.multiple_of(b * 256, 256), 256)
             for a in range(2):
                 block = d_x[a].reshape(PARTNERS * ENC_MAX, piece)
-                mem_v[a, at, c * piece : (c + 1) * piece] = matmul(
+                mg_out[a, at, c * piece : (c + 1) * piece] = matmul(
                     grad_m[at, :], block, NN
                 ).astype(BF16)
-
-        grad_copy(c).start()
 
     def finish(c):
         @pl.loop(0, PARTNERS)
@@ -306,23 +334,22 @@
         grad_m[b * 256 : (b + 1) * 256, :] = one_hot(hits)
 
     expand(1)
-    for c in range(2, CHUNKS):
+    for c in range(2, chunks):
         pack(c)
         expand(c)
-    for c in range(CHUNKS):
+    for c in range(chunks):
         attend(c)
         collect(c)
         if c:
             finish(c - 1)
-    finish(CHUNKS - 1)
-
-    for c in range(CHUNKS):
+    finish(chunks - 1)
+
+    for c in range(chunks):
         for a in range(2):
             for step in range(1, tensors):
                 first_copy(c, a, step).wait_send()
                 last_copy(c, a, step).wait()
             last_copy(c, a, 0).wait()
-        grad_copy(c).wait()
 
         @pl.loop(0, PARTNERS)
         def _(slot):
@@ -334,53 +361,56 @@
     enc_count, width = memory.shape[1:]
     rows = queries.shape[0]
     dec_count = rows * tensors
-    piece = width // CHUNKS
-    blocks = (CHUNKS, 2, PARTNERS, DEC_MAX, piece)
+    chunks = chunk_count(width)
+    piece = width // chunks
+    blocks = (chunks, 2, PARTNERS, DEC_MAX, piece)
     peers = max(tensors - 1, 1)
+    scalars = (enc_lengths.T, dec_lengths.T, readers.T)
     anywhere = pl.BlockSpec(memory_space=pl.ANY)
-    scalars = pl.BlockSpec(memory_space=pltpu.SMEM)
+    resident = pl.BlockSpec(memory_space=pltpu.VMEM)
     dma = pltpu.SemaphoreType.DMA
     return pl.pallas_call(
         functools.partial(kernel, sections, tensors),
         out_shape=(
-            jax.ShapeDtypeStruct(queries.shape, BF16),
-            jax.ShapeDtypeStruct(queries.shape, BF16),
-            jax.ShapeDtypeStruct(memory.shape, BF16),
+            pltpu.VMEM(queries.shape, BF16),
+            pltpu.VMEM(queries.shape, BF16),
+            pltpu.VMEM(memory.shape, BF16),
         ),
-        in_specs=[anywhere] * 3 + [scalars] * 3,
-        out_specs=(anywhere,) * 3,
+        in_specs=[anywhere] * 6,
+        out_specs=(resident,) * 3,
         scratch_shapes=[
             pltpu.VMEM((2, enc_count, width), BF16),
-            pltpu.VMEM((CHUNKS, 2, dec_count, piece), BF16),
+            pltpu.VMEM((chunks, 2, dec_count, piece), BF16),
             pltpu.VMEM(blocks, BF16),
             pltpu.VMEM(blocks, BF16),
             pltpu.VMEM(blocks, BF16),
             pltpu.VMEM(blocks, BF16),
-            pltpu.VMEM((CHUNKS, 2, dec_count, piece), BF16),
-            pltpu.VMEM((CHUNKS, 2, PARTNERS, ENC_MAX, piece), BF16),
+            pltpu.VMEM((chunks, 2, dec_count, piece), BF16),
+            pltpu.VMEM((chunks, 2, PARTNERS, ENC_MAX, piece), BF16),
             pltpu.VMEM((2, PARTNERS, ENC_MAX, piece), BF16),
             pltpu.VMEM((2, PARTNERS // 2 * DEC_MAX, dec_count), BF16),
             pltpu.VMEM((dec_count, PARTNERS * DEC_MAX), BF16),
             pltpu.VMEM((PARTNERS // 2, 2 * ENC_MAX, enc_count), BF16),
             pltpu.VMEM((enc_count, PARTNERS * ENC_MAX), BF16),
+            *[pltpu.SMEM(array.shape, jnp.int32) for array in scalars],
             pltpu.SMEM((4, PARTNERS), jnp.int32),
-            dma((CHUNKS, 2, peers)),
-            dma((CHUNKS, 2, peers)),
-            dma((CHUNKS, 2)),
-            dma((CHUNKS, PARTNERS)),
-            dma((CHUNKS, PARTNERS)),
-            dma((CHUNKS, PARTNERS)),
-            dma((CHUNKS, PARTNERS)),
-            dma((CHUNKS, 2, peers)),
-            dma((CHUNKS, 2, peers)),
-            dma((CHUNKS, 2)),
+            dma((chunks, 2, peers)),
+            dma((chunks, 2, peers)),
+            dma((chunks, 2)),
+            dma((chunks, PARTNERS)),
+            dma((chunks, PARTNERS)),
+            dma((chunks, PARTNERS)),
+            dma((chunks, PARTNERS)),
+            dma((chunks, 2, peers)),
+            dma((chunks, 2, peers)),
+            dma((chunks, 2)),
             dma,
-            dma((CHUNKS,)),
+            dma((3,)),
         ],
         compiler_params=pltpu.CompilerParams(
-            collective_id=0, has_side_effects=True, vmem_limit_bytes=60 * 1024 * 1024
+            collective_id=0, has_side_effects=True, vmem_limit_bytes=46 * 1024 * 1024
         ),
-    )(memory, queries, out_grad, enc_lengths, dec_lengths, readers)
+    )(memory, queries, out_grad, *scalars)
 
 
 def solution(mesh):

time: 220 us -> 208 us (0.945); the launches traced: 220 us -> 204 us
  local copies, waits for them, and re-layouts: 15.3 us -> 4.64 us
  Pallas kernels: 204 us -> 198 us
    unnamed x6 -> x3, local copies, waits for them, and re-layouts: 15.3 us -> 4.64 us
    pallas_call x1, Pallas kernels: 204 us -> 198 us  [body(): pl.pallas_call(functools.partial(kernel, sections, tensors), out_shape=(p...]
where the time goes in v2:
time: 208 us; the launch traced here: 204 us
  Pallas kernels  198 us (95%)
  local copies, waits for them, and re-layouts  4.64 us (2%)
    pallas_call x1, Pallas kernels, body(): pl.pallas_call(functools.partial(kernel, sections, tensors), out_shape=(p...  198 us
    unnamed x3, local copies, waits for them, and re-layouts  4.64 us

profile of v2, /device:TPU:15, one launch (start us, length us, event | category | flops | bytes accessed | tf_op | source)
XLA Modules:
  0.0 203.7 jit_solution(7066453501782795474)
XLA Ops:
  0.6 198.4 %shard_map.85 = (bf16[128,4096]{1,0:T(8,128)(2,1)S(1)}, bf16[128,4096]{1,0:T(8,128)(2,1)S(1)}, bf16[2,768,2048]{2,1,0:T(8,128)(2,1)S(1)}) custom-call(bf16[2,768,2048]{2,1,0:T(8,128)(2,1)} %mem_hbm.1, bf16[128,4096]{1,0:T(8,128)(2,1)} %q_hbm.1, bf16[128,4096]{1,0:T(8,128)(2,1)} %g_hbm.1, s32[8,16]{1,0:T(8,128)} %bitcast.3, s32[8,16]{1,0:T(8,128)} %bitcast.4, ...), custom_call_target="tpu_custom_call" | custom-call | tf_op jit(solution)/shard_map/pallas_call | solution.py:372
  199.0 1.0 copy.12
  200.0 1.0 copy.13
  201.0 2.7 %copy.14 = bf16[2,768,2048]{2,1,0:T(8,128)(2,1)} copy(bf16[2,768,2048]{2,1,0:T(8,128)(2,1)S(1)} %get-tuple-element.5) | data formatting | bytes 12582912

commit v3 on v2

--- a/solution.py
+++ b/solution.py
@@ -91,18 +91,6 @@
 
     half = PARTNERS // 2
 
-    def rank_at(turn):
-        other = lax.rem(lax.div(turn, half) + 1 + lax.div(2 * me, sections), 2)
-        return other * half + lax.rem(turn + lax.div(me, spacing), half)
-
-    def holder_slot(turn):
-        holder = lax.rem(me + sections - 1, spacing) + spacing * rank_at(turn)
-        return lax.div(lax.rem(me + sections - holder - 1 + sections, sections), spacing)
-
-    def reader_slot(turn):
-        reader = lax.rem(me + 1, spacing) + spacing * rank_at(turn)
-        return lax.div(lax.rem(reader + 2 * sections - me - 1, sections), spacing)
-
     def peer_of(step):
         return lax.rem(mine + step, tensors)
 
@@ -250,7 +238,7 @@
 
         @pl.loop(0, PARTNERS)
         def _(turn):
-            forward_copy(c, holder_slot(jnp.int32(turn))).start()
+            forward_copy(c, turn).start()
 
     def expand(c):
         @pl.loop(0, PARTNERS // 2)
@@ -262,7 +250,7 @@
     def attend(c):
         @pl.loop(0, PARTNERS)
         def _(turn):
-            slot = reader_slot(jnp.int32(turn))
+            slot = turn
             forward_copy(c, slot).wait_recv()
             valid = iota((DEC_MAX, ENC_MAX), 1) < meta[3, slot]
             for h in range(piece // HD):
@@ -305,6 +293,17 @@
             for step in list(range(1, tensors)) + [0]:
                 last_copy(c, a, step).start()
 
+    def settle():
+        for c in range(chunks):
+            for a in range(2):
+                for step in range(1, tensors):
+                    first_copy(c, a, step).wait_send()
+
+            @pl.loop(0, PARTNERS)
+            def _(slot):
+                forward_copy(c, slot).wait_send()
+                back_copy(c, slot).wait_send()
+
     pack(0)
 
     for slot in range(PARTNERS):
@@ -340,21 +339,18 @@
     for c in range(chunks):
         attend(c)
         collect(c)
-        if c:
-            finish(c - 1)
-    finish(chunks - 1)
+        if c >= 3:
+            finish(c - 3)
+    for c in range(max(chunks - 3, 0), chunks):
+        if c == chunks - 1:
+            settle()
+        finish(c)
 
     for c in range(chunks):
         for a in range(2):
             for step in range(1, tensors):
-                first_copy(c, a, step).wait_send()
                 last_copy(c, a, step).wait()
             last_copy(c, a, 0).wait()
-
-        @pl.loop(0, PARTNERS)
-        def _(slot):
-            forward_copy(c, slot).wait_send()
-            back_copy(c, slot).wait_send()
 
 
 def body(sections, tensors, memory, queries, out_grad, enc_lengths, dec_lengths, readers):

time: 208 us -> 204 us (0.981); the launches traced: 204 us -> 204 us
  no operation moved by 1% of the time
where the time goes in v3:
time: 204 us
  Pallas kernels  199 us (98%)
  local copies, waits for them, and re-layouts  4.64 us (2%)
    pallas_call x1, Pallas kernels, body(): pl.pallas_call(functools.partial(kernel, sections, tensors), out_shape=(p...  199 us
    unnamed x3, local copies, waits for them, and re-layouts  4.64 us

profile of v3, /device:TPU:15, one launch (start us, length us, event | category | flops | bytes accessed | tf_op | source)
XLA Modules:
  0.0 203.8 jit_solution(8989292422375216619)
XLA Ops:
  0.6 198.5 %shard_map.85 = (bf16[128,4096]{1,0:T(8,128)(2,1)S(1)}, bf16[128,4096]{1,0:T(8,128)(2,1)S(1)}, bf16[2,768,2048]{2,1,0:T(8,128)(2,1)S(1)}) custom-call(bf16[2,768,2048]{2,1,0:T(8,128)(2,1)} %mem_hbm.1, bf16[128,4096]{1,0:T(8,128)(2,1)} %q_hbm.1, bf16[128,4096]{1,0:T(8,128)(2,1)} %g_hbm.1, s32[8,16]{1,0:T(8,128)} %bitcast.3, s32[8,16]{1,0:T(8,128)} %bitcast.4, ...), custom_call_target="tpu_custom_call" | custom-call | tf_op jit(solution)/shard_map/pallas_call | solution.py:368
  199.2 1.0 copy.12
  200.2 1.0 copy.13
  201.1 2.7 %copy.14 = bf16[2,768,2048]{2,1,0:T(8,128)(2,1)} copy(bf16[2,768,2048]{2,1,0:T(8,128)(2,1)S(1)} %get-tuple-element.5) | data formatting | bytes 12582912
